TPU v7x, 256 devices: a whole 4x4x8 slice. The times are simulated.
256 devices in a mesh: req: 8 (over y, core), ep: 32 (over x, z).
Axes of the slice: x: 4, y: 4, z: 8, core: 2. Of those that a mesh axis runs over, the one named last changes fastest.
Arguments:
- queries: bfloat16 [2048, 64, 576], P(('req', 'ep')), may hold values from -7 to 7
- latent_cache: bfloat16 [256, 512, 576], P(('req', 'ep')), may hold values from -3 to 3
- new_latents: bfloat16 [2048, 576], P(('req', 'ep')), may hold values from -4 to 4
- parents: int32 [128, 16], replicated, may hold values from 0 to 14, as said below
- cache_len: int32 [128], replicated, may hold values from 128 to 1024
- tokens: bfloat16 [2048, 7168], P(('req', 'ep')), may hold values from -6 to 6
- route_ids: int32 [2048, 8], P(('req', 'ep')), may hold values from 0 to 31, all different within a row; in each aligned block of 8 rows (0 to 7, 8 to 15, ...) at most 3 rows name the same one
- route_scores: float32 [2048, 8], P(('req', 'ep')), may hold values from 0.05 to 1
- w_gate: bfloat16 [32, 7168, 2048], P('ep', None, 'req'), may hold values from -0.0625 to 0.0625
- w_up: bfloat16 [32, 7168, 2048], P('ep', None, 'req'), may hold values from -0.0625 to 0.0625
- w_down: bfloat16 [32, 2048, 7168], P('ep', 'req'), may hold values from -0.125 to 0.125
Outputs:
- attention_out: bfloat16 [2048, 64, 512], P(('req', 'ep'))
- moe_out: bfloat16 [2048, 7168], P(('req', 'ep'))
Inputs may be any that keep to these rules, and one draw needn't show every extreme that they name: `route_ids`: each row names 8 different experts. Among the 8 tokens of one device (aligned blocks of 8 rows) no expert is named by more than 3 tokens, a bound that some block reaches. parents[q, 0] = 0 and parents[q, j] < j for j >= 1.
All inputs are finite; a program needn't handle non-finite values.
Results may differ from a plain program's by a relative error of at most 0.015.
Values may be sent and summed in bfloat16 or wider, within the bound.
A program may use at most 128 MiB of HBM per device.

v0:
```python
import jax
import jax.numpy as jnp
from jax import lax
from jax.sharding import PartitionSpec as P

VDIM = 512
score_scale = 192.0 ** (-0.5)
route_scale = 2.5


def partner(block, axis, stride):
    count = lax.axis_size(axis)
    route = []
    for low in range(count):
        high = low | 1 << stride
        if high != low and high < count:
            route += [(low, high), (high, low)]
    return lax.ppermute(block, axis, route)


def ancestor_table(parent_row):
    node_count = parent_row.shape[0]
    node_ids = jnp.arange(node_count, dtype=jnp.int32)
    current = node_ids
    visible = node_ids[:, None] == node_ids[None, :]
    for repeat in range(node_count):
        current = parent_row[current]
        visible = visible | (current[:, None] == node_ids[None, :])
    return visible


def expert_mlp(row_block, w_gate, w_up, w_down):
    gate_val = jnp.dot(row_block, w_gate[0], preferred_element_type=jnp.float32)
    up_val = jnp.dot(row_block, w_up[0], preferred_element_type=jnp.float32)
    hidden = (jax.nn.silu(gate_val) * up_val).astype(jnp.bfloat16)
    return jnp.dot(hidden, w_down[0], preferred_element_type=jnp.float32).astype(jnp.bfloat16)


def body(
    queries,
    latent_cache,
    new_latents,
    parents,
    cache_len,
    tokens,
    route_ids,
    route_scores,
    w_gate,
    w_up,
    w_down,
):
    ep_count = lax.axis_size("ep")
    position = lax.axis_index("req") * ep_count + lax.axis_index("ep")
    request = position // 2
    half_index = position % 2
    tok_dev = tokens.shape[0]
    model_width = tokens.shape[1]
    other_cache, other_fresh = partner((latent_cache, new_latents), "ep", 0)
    lower_half = half_index == 0
    cache_rows = jnp.concatenate(
        [
            jnp.where(lower_half, latent_cache[0], other_cache[0]),
            jnp.where(lower_half, other_cache[0], latent_cache[0]),
        ],
        axis=0,
    )
    fresh_rows = jnp.concatenate(
        [
            jnp.where(lower_half, new_latents, other_fresh),
            jnp.where(lower_half, other_fresh, new_latents),
        ],
        axis=0,
    )
    key_rows = jnp.concatenate([cache_rows, fresh_rows], axis=0)
    context = cache_rows.shape[0]
    parent_row = lax.dynamic_index_in_dim(parents, request, 0, keepdims=False)
    tree_vis = lax.dynamic_slice_in_dim(
        ancestor_table(parent_row), half_index * tok_dev, tok_dev, 0
    )
    length = lax.dynamic_index_in_dim(cache_len, request, 0, keepdims=False)
    cached = jnp.arange(context, dtype=jnp.int32) < length
    visible = jnp.concatenate(
        [jnp.broadcast_to(cached[None, :], (tok_dev, context)), tree_vis], axis=1
    )
    head_count = queries.shape[1]
    flat_query = queries.reshape(tok_dev * head_count, queries.shape[2])
    scores = (
        lax.dot_general(
            flat_query, key_rows, (((1,), (1,)), ((), ())), preferred_element_type=jnp.float32
        )
        * score_scale
    )
    scores = scores.reshape(tok_dev, head_count, key_rows.shape[0])
    masked = jnp.where(visible[:, None, :], scores, -jnp.inf)
    row_max = jnp.max(masked, axis=-1, keepdims=True)
    shifted = jnp.exp(masked - row_max)
    attn_probs = (shifted / jnp.sum(shifted, axis=-1, keepdims=True)).astype(jnp.bfloat16)
    value_rows = key_rows[:, :VDIM]
    attended = jnp.dot(
        attn_probs.reshape(tok_dev * head_count, key_rows.shape[0]),
        value_rows,
        preferred_element_type=jnp.float32,
    )
    attention_out = attended.reshape(tok_dev, head_count, VDIM).astype(jnp.bfloat16)
    top_count = route_ids.shape[1]
    capacity = min(tok_dev, tok_dev * top_count // ep_count + 1)
    route_weight = route_scale * route_scores / jnp.sum(route_scores, axis=1, keepdims=True)
    pair_ids = route_ids.reshape(-1)
    onehot = (pair_ids[:, None] == jnp.arange(ep_count, dtype=jnp.int32)[None, :]).astype(jnp.int32)
    slot_rank = jnp.sum(jnp.cumsum(onehot, axis=0) * onehot, axis=1) - 1
    slot_of = (pair_ids * capacity + slot_rank).reshape(tok_dev, top_count)
    slot_ids = jnp.arange(ep_count * capacity, dtype=jnp.int32)
    slot_hits = slot_of[None, :, :] == slot_ids[:, None, None]
    dispatch = jnp.any(slot_hits, axis=2).astype(jnp.bfloat16)
    combine = jnp.sum(jnp.where(slot_hits, route_weight[None, :, :], 0.0), axis=2)
    outgoing = jnp.dot(dispatch, tokens, preferred_element_type=jnp.float32).astype(jnp.bfloat16)
    outgoing = outgoing.reshape(ep_count, capacity, model_width)
    arrived = lax.all_to_all(outgoing, "ep", split_axis=0, concat_axis=0, tiled=True)
    partial_value = expert_mlp(
        lax.all_gather(
            arrived.reshape(ep_count * capacity, model_width), "req", axis=0, tiled=True
        ),
        w_gate,
        w_up,
        w_down,
    )
    summed = lax.psum_scatter(
        partial_value.astype(jnp.float32).astype(jnp.bfloat16),
        "req",
        scatter_dimension=0,
        tiled=True,
    ).astype(jnp.float32)
    summed = summed.reshape(ep_count, capacity, model_width)
    returned = lax.all_to_all(
        summed.astype(jnp.bfloat16), "ep", split_axis=0, concat_axis=0, tiled=True
    ).astype(summed.dtype)
    moe_out = lax.dot_general(
        combine,
        returned.reshape(ep_count * capacity, model_width),
        (((0,), (0,)), ((), ())),
        precision=lax.Precision.HIGHEST,
        preferred_element_type=jnp.float32,
    )
    return (attention_out, moe_out.astype(jnp.bfloat16))


def solution(mesh):
    placed = (
        P(("req", "ep"), None, None),
        P(("req", "ep"), None, None),
        P(("req", "ep"), None),
        P(),
        P(),
        P(("req", "ep"), None),
        P(("req", "ep"), None),
        P(("req", "ep"), None),
        P("ep", None, "req"),
        P("ep", None, "req"),
        P("ep", "req", None),
    )
    return jax.shard_map(
        body,
        mesh=mesh,
        in_specs=placed,
        out_specs=(P(("req", "ep"), None, None), P(("req", "ep"), None)),
        check_vma=False,
    )
```

profile of v0, /device:TPU:32, one launch (start us, length us, event | category | flops | bytes accessed | tf_op | source)
XLA Modules:
  0.0 299.1 jit_solution(5161164357514581001)
XLA Ops:
  7.2 0.0 all-gather.2.cloned.1.call-start
  7.2 0.8 eq.306
  8.0 0.1 fusion.36
  8.1 0.1 reduce_window_sum.11
  8.2 0.2 select_reduce_fusion.1
  8.4 0.1 sub.24
  8.5 0.7 multiply_add_fusion
  9.2 0.1 fusion.35
  9.3 2.5 convolution_convert_fusion.1
  11.8 2.6 reshape.271
  14.5 56.6 %all_to_all.10 = bf16[32,3,7168]{2,1,0:T(4,128)(2,1)} all-to-all(bf16[32,3,7168]{2,1,0:T(4,128)(2,1)S(1)} %reshape.271), channel_id=1, replica_groups=mesh['req'=8,'ep'=32] {'ep'}, dimensions={0} | all-to-all | bytes 2752512 | tf_op jit(solution)/shard_map/all_to_all | solution.py:118
  71.1 4.1 %reshape.272 = bf16[96,7168]{1,0:T(8,128)(2,1)} reshape(bf16[32,3,7168]{2,1,0:T(4,128)(2,1)} %all_to_all.10) | data formatting | bytes 2752512 | tf_op jit(solution)/shard_map/reshape | solution.py:121
  75.3 0.0 reduce-scatter.2.cloned.1.call-start
  75.3 59.8 %all-gather.2.cloned.1.call-done = bf16[768,7168]{1,0:T(8,128)(2,1)} async-done(((bf16[96,7168]{1,0:T(8,128)(2,1)}), bf16[768,7168]{1,0:T(8,128)(2,1)}) %all-gather.2.cloned.1.call-update) | async-done | bytes 11010064 | tf_op jit(solution)/shard_map/all_gather | solution.py:120
  135.2 6.9 %fusion.3 = f32[768,256]{1,0:T(8,128)S(1)} fusion(bf16[768,7168]{1,0:T(8,128)(2,1)} %all-gather.2.cloned.1.call-done, bf16[1,7168,256]{2,1,0:T(8,128)(2,1)} %param.19), kind=kOutput, calls=%fused_computation.22 | convolution fusion | flops 2818572288 | bytes 15466496 | tf_op jit(solution)/shard_map/dot_general | solution.py:33
  142.0 18.9 %convolution_convert_fusion = bf16[768,7168]{1,0:T(8,128)(2,1)} fusion(bf16[1,256,7168]{2,1,0:T(8,128)(2,1)} %param.21, bf16[768,7168]{1,0:T(8,128)(2,1)} %all-gather.2.cloned.1.call-done, bf16[1,7168,256]{2,1,0:T(8,128)(2,1)} %param.20, f32[768,256]{1,0:T(8,128)S(1)} %fusion.3), kind=kOutput, calls=%fused_computation.16 | convolution fusion | flops 5643829248 | bytes 30146560 | tf_op jit(solution)/shard_map/dot_general | solution.py:36
  161.0 0.6 collective-permute-start
  161.6 0.1 copy-done.6
  161.7 1.4 collective-permute-start.1
  163.1 0.2 dynamic-slice_reduce_fusion
  163.3 0.7 gather_fusion
  164.0 0.7 gather_fusion.1
  164.7 0.7 gather_fusion.2
  165.4 0.7 gather_fusion.3
  166.0 0.7 gather_fusion.4
  166.7 0.7 gather_fusion.5
  167.4 0.7 gather_fusion.6
  168.1 0.7 gather_fusion.7
  168.8 0.7 gather_fusion.8
  169.5 0.7 gather_fusion.9
  170.2 0.7 gather_fusion.10
  170.8 0.7 gather_fusion.11
  171.5 0.1 dynamic-slice
  171.6 0.7 gather_fusion.12
  172.3 0.1 dynamic-slice.1
  172.4 0.7 gather_fusion.13
  173.0 0.1 dynamic-slice.2
  173.1 0.7 gather_fusion.14
  173.8 0.1 dynamic-slice.3
  173.9 0.7 gather_fusion.15
  174.5 0.1 dynamic-slice.4
  174.6 0.6 dynamic_slice.11
  175.2 0.6 iota_compare_fusion.19
  175.9 0.1 iota_compare_fusion.2
  176.0 0.1 fusion.51
  176.1 52.9 %reduce-scatter.2.cloned.1.call-done = bf16[96,7168]{1,0:T(8,128)(2,1)} async-done(((bf16[768,7168]{1,0:T(8,128)(2,1)}), bf16[96,7168]{1,0:T(8,128)(2,1)}) %reduce-scatter.2.cloned.1.call-update) | async-done | bytes 1376272 | tf_op jit(solution)/shard_map/reduce_scatter | solution.py:127
  229.0 4.0 %convert_element_type.37 = bf16[32,3,7168]{2,1,0:T(4,128)(2,1)} reshape(bf16[96,7168]{1,0:T(8,128)(2,1)} %reduce-scatter.2.cloned.1.call-done) | data formatting | bytes 2752512 | tf_op jit(solution)/shard_map/convert_element_type | solution.py:135
  232.9 10.2 %all-to-all-start.1 = ((bf16[32,3,7168]{2,1,0:T(4,128)(2,1)}), bf16[32,3,7168]{2,1,0:T(4,128)(2,1)S(1)}, u32[]{:S(2)}, u32[]{:S(2)}) async-start(bf16[32,3,7168]{2,1,0:T(4,128)(2,1)} %convert_element_type.37), calls=%async_computation.2 | async-start | bytes 3670016 | tf_op jit(solution)/shard_map/all_to_all | solution.py:134
  243.1 0.1 reduce_sum.38
  243.3 0.1 multiply_divide_fusion
  243.3 0.7 select_reduce_fusion
  244.0 1.4 copy.28
  245.4 1.0 broadcast_in_dim.21
  246.4 2.4 copy.32
  248.8 2.2 copy.29
  251.0 1.3 select_bitcast_fusion.1
  252.3 1.1 fusion.70
  253.5 0.4 fusion.7
  253.9 0.4 divide_convert_fusion
  254.2 1.4 copy.33
  255.6 3.2 %convolution_convert_fusion.3 = bf16[8,64,512]{2,1,0:T(8,128)(2,1)} fusion(bf16[8,64,1040]{2,1,0:T(8,128)(2,1)} %bitcast.100, bf16[8,576]{1,0:T(8,128)(2,1)} %copy-done.8, bf16[8,576]{1,0:T(8,128)(2,1)} %copy-done.7, bf16[512,576]{1,0:T(8,128)(2,1)} %copy-done.2, bf16[512,576]{1,0:T(8,128)(2,1)} %copy-done.1), kind=kOutput, calls=%fused_computation.37 | convolution fusion | flops 549781504 | bytes 2787328 | tf_op jit(solution)/shard_map/dot_general | solution.py:99
  258.8 28.4 %all-to-all-done.1 = bf16[32,3,7168]{2,1,0:T(4,128)(2,1)S(1)} async-done(((bf16[32,3,7168]{2,1,0:T(4,128)(2,1)}), bf16[32,3,7168]{2,1,0:T(4,128)(2,1)S(1)}, u32[]{:S(2)}, u32[]{:S(2)}) %all-to-all-start.1) | async-done | bytes 1376288 | tf_op jit(solution)/shard_map/all_to_all | solution.py:134
  287.2 2.4 reshape.273
  289.6 2.6 convolution_convert_fusion.2
  (61 shorter events, 0.3 us)
Async XLA Ops:
  7.2 245.1 %copy-start = (bf16[8,64,576]{2,1,0:T(8,128)(2,1)S(1)}, bf16[8,64,576]{2,1,0:T(8,128)(2,1)}, u32[]{:S(2)}) copy-start(bf16[8,64,576]{2,1,0:T(8,128)(2,1)} %param.11) | copy-start | bytes 1769476
  7.2 128.0 %all-gather.2.cloned.1.call-start = ((), (), s32[]{:S(2)}) async-start(), calls=%async_computation.3 | async-start | bytes 12386304 | tf_op jit(solution)/shard_map/all_gather | solution.py:120
  75.3 153.7 %reduce-scatter.2.cloned.1.call-start = ((), (), s32[]{:S(2)}) async-start(), calls=%async_computation.4 | async-start | bytes 12386304 | tf_op jit(solution)/shard_map/reduce_scatter | solution.py:127
  161.0 0.7 copy-start.6
  161.0 2.1 copy-start.9
  161.0 87.8 %collective-permute-start = (bf16[1,512,576]{1,2,0:T(8,128)(2,1)}, bf16[1,512,576]{1,2,0:T(8,128)(2,1)}, u32[]{:S(2)}, u32[]{:S(2)}) collective-permute-start(bf16[1,512,576]{1,2,0:T(8,128)(2,1)} %param.12), channel_id=1, source_target_pairs={{0,1},{1,0},{2,3},{3,2},{4,5},{5,4},{6,7},{7,6},{8,9},{9,8},{10,11... | collective-permute-start | bytes 1769480 | tf_op jit(solution)/shard_map/ppermute | solution.py:18
  161.7 87.1 %collective-permute-start.1 = (bf16[8,576]{1,0:T(8,128)(2,1)S(1)}, bf16[8,576]{1,0:T(8,128)(2,1)S(1)}, u32[]{:S(2)}, u32[]{:S(2)}) collective-permute-start(bf16[8,576]{1,0:T(8,128)(2,1)S(1)} %copy-done.6), channel_id=1, source_target_pairs={{0,1},{1,0},{2,3},{3,2},{4,5},{5,4},{6,7},{7,6},{8,9},{9,8},{10,11... | collective-permute-start | bytes 27656 | tf_op jit(solution)/shard_map/ppermute | solution.py:18
  168.8 5.8 %copy-start.10 = (s32[128]{0:T(128)S(1)}, s32[128]{0:T(128)}, u32[]{:S(2)}) copy-start(s32[128]{0:T(128)} %param.15) | copy-start | bytes 1540
  232.9 10.2 %copy-start.5 = (f32[8,8]{1,0:T(8,128)S(1)}, f32[8,8]{1,0:T(8,128)}, u32[]{:S(2)}) copy-start(f32[8,8]{1,0:T(8,128)} %param.18) | copy-start | bytes 772
  232.9 54.3 %all-to-all-start.1 = ((bf16[32,3,7168]{2,1,0:T(4,128)(2,1)}), bf16[32,3,7168]{2,1,0:T(4,128)(2,1)S(1)}, u32[]{:S(2)}, u32[]{:S(2)}) async-start(bf16[32,3,7168]{2,1,0:T(4,128)(2,1)} %convert_element_type.37), calls=%async_computation.2 | async-start | bytes 3670016 | tf_op jit(solution)/shard_map/all_to_all | solution.py:134
  248.8 4.7 %copy-start.7 = (bf16[8,576]{1,0:T(8,128)(2,1)}, bf16[8,576]{1,0:T(8,128)(2,1)S(1)}, u32[]{:S(2)}) copy-start(bf16[8,576]{1,0:T(8,128)(2,1)S(1)} %get-tuple-element.4) | copy-start | bytes 27652
  248.8 4.7 %copy-start.8 = (bf16[8,576]{1,0:T(8,128)(2,1)}, bf16[8,576]{1,0:T(8,128)(2,1)S(1)}, u32[]{:S(2)}) copy-start(bf16[8,576]{1,0:T(8,128)(2,1)S(1)} %get-tuple-element.5) | copy-start | bytes 27652
  251.0 1.3 copy-start.3
  252.3 1.2 copy-start.1
  252.3 1.2 copy-start.2
  258.8 30.7 %copy-start.4 = (f32[96,8]{0,1:T(8,128)S(1)}, f32[96,8]{0,1:T(8,128)}, u32[]{:S(2)}) copy-start(f32[96,8]{0,1:T(8,128)} %select_reduce_fusion) | copy-start | bytes 9220
Sparse Core Ops, SparseCore 0:
  75.4 59.7 all-gather.1
  161.1 67.8 reduce-scatter.1
where the time goes:
time: 300 us; the launch traced here: 299 us
  waiting for transfers between devices  141 us (47%)
  blocking collectives  56.6 us (19%)
  matrix products  35.4 us (12%)
  local copies, waits for them, and re-layouts  34.2 us (11%)
  between operations  14.4 us (5%)
  starting transfers between devices  12.2 us (4%)
  other arithmetic  5.09 us (2%)
    all_gather x1, waiting for transfers between devices, body(): lax.all_gather(arrived.reshape(ep_count * capacity, model_width), 'req',...  59.8 us
    all_to_all x1, blocking collectives, body(): lax.all_to_all(outgoing, 'ep', split_axis=0, concat_axis=0, tiled=True)  56.6 us
    reduce_scatter x1, waiting for transfers between devices, body(): lax.psum_scatter(partial_value.astype(jnp.float32).astype(jnp.bfloat16),...  52.9 us
    all_to_all x1, waiting for transfers between devices, body(): lax.all_to_all(summed.astype(jnp.bfloat16), 'ep', split_axis=0, concat_ax...  28.4 us
    dot_general x1, matrix products, expert_mlp(): jnp.dot(hidden, w_down[0], preferred_element_type=jnp.float32)  18.9 us
    gather x16, local copies, waits for them, and re-layouts, ancestor_table(): current = parent_row[current]  10.5 us
    all_to_all x1, starting transfers between devices, body(): lax.all_to_all(summed.astype(jnp.bfloat16), 'ep', split_axis=0, concat_ax...  10.2 us
    dot_general x1, matrix products, expert_mlp(): gate_val = jnp.dot(row_block, w_gate[0], preferred_element_type=jnp.float32)  6.88 us
  transfers between devices with their start and end apart: 5, of which 3 were waited for; matrix products, arithmetic and copies ran while one was open for 11% of the time, Pallas kernels for 0%

commit v1 on v0

--- a/solution.py
+++ b/solution.py
@@ -117,8 +117,16 @@
     outgoing = outgoing.reshape(ep_count, capacity, model_width)
     arrived = lax.all_to_all(outgoing, "ep", split_axis=0, concat_axis=0, tiled=True)
     partial_value = expert_mlp(
-        lax.all_gather(
-            arrived.reshape(ep_count * capacity, model_width), "req", axis=0, tiled=True
+        jnp.concatenate(
+            lax.all_to_all(
+                jnp.stack(
+                    [arrived.reshape(ep_count * capacity, model_width)] * lax.axis_size("req")
+                ),
+                "req",
+                0,
+                0,
+            ),
+            axis=0,
         ),
         w_gate,
         w_up,

time: 300 us -> 368 us (1.23)
  blocking collectives: 56.6 us -> 186 us
  waiting for transfers between devices: 141 us -> 74.8 us
  local copies, waits for them, and re-layouts: 34.2 us -> 43.1 us
  matrix products: 35.4 us -> 31.5 us
    all_to_all x0 -> x1, blocking collectives: none -> 129 us  [body(): lax.all_to_all(jnp.stack([arrived.reshape(ep_count * capacity, model_widt...]
    all_gather x1 -> x0, waiting for transfers between devices: 59.8 us -> none  [body(): lax.all_gather(arrived.reshape(ep_count * capacity, model_width), 'req',...]
    another operation x0 -> x2, local copies, waits for them, and re-layouts: none -> 8.51 us  [body(): jnp.stack([arrived.reshape(ep_count * capacity, model_width)] * lax.axis_...]
    reduce_scatter x1, waiting for transfers between devices: 52.9 us -> 46.4 us  [body(): lax.psum_scatter(partial_value.astype(jnp.float32).astype(jnp.bfloat16),...]
    unnamed x23 -> x27, local copies, waits for them, and re-layouts: 1.52 us -> 6.11 us
    reshape x1 -> x0, local copies, waits for them, and re-layouts: 4.14 us -> none  [body(): arrived.reshape(ep_count * capacity, model_width)]
    dot_general x1, matrix products: 6.88 us -> 3 us  [expert_mlp(): gate_val = jnp.dot(row_block, w_gate[0], preferred_element_type=jnp.float32)]
  transfers between devices with their start and end apart: 5 -> 4, of which waited for: 3 -> 2; matrix products, arithmetic and copies ran while one was open for 11% -> 9% of each run, Pallas kernels for 0% -> 0%
where the time goes in v1:
time: 368 us; the launch traced here: 367 us
  blocking collectives  186 us (51%)
  waiting for transfers between devices  74.8 us (20%)
  local copies, waits for them, and re-layouts  43.1 us (12%)
  matrix products  31.5 us (9%)
  between operations  14.4 us (4%)
  starting transfers between devices  12.2 us (3%)
  other arithmetic  5.1 us (1%)
    all_to_all x1, blocking collectives, body(): lax.all_to_all(jnp.stack([arrived.reshape(ep_count * capacity, model_widt...  129 us
    all_to_all x1, blocking collectives, body(): lax.all_to_all(outgoing, 'ep', split_axis=0, concat_axis=0, tiled=True)  56.6 us
    reduce_scatter x1, waiting for transfers between devices, body(): lax.psum_scatter(partial_value.astype(jnp.float32).astype(jnp.bfloat16),...  46.4 us
    all_to_all x1, waiting for transfers between devices, body(): lax.all_to_all(summed.astype(jnp.bfloat16), 'ep', split_axis=0, concat_ax...  28.4 us
    dot_general x1, matrix products, expert_mlp(): jnp.dot(hidden, w_down[0], preferred_element_type=jnp.float32)  18.9 us
    gather x16, local copies, waits for them, and re-layouts, ancestor_table(): current = parent_row[current]  10.5 us
    all_to_all x1, starting transfers between devices, body(): lax.all_to_all(summed.astype(jnp.bfloat16), 'ep', split_axis=0, concat_ax...  10.2 us
    another operation x2, local copies, waits for them, and re-layouts, body(): jnp.stack([arrived.reshape(ep_count * capacity, model_width)] * lax.axis_...  8.51 us
  transfers between devices with their start and end apart: 4, of which 2 were waited for; matrix products, arithmetic and copies ran while one was open for 9% of the time, Pallas kernels for 0%

profile of v1, /device:TPU:32, one launch (start us, length us, event | category | flops | bytes accessed | tf_op | source)
XLA Modules:
  0.0 366.9 jit_solution(14014648368198775701)
XLA Ops:
  7.2 0.8 eq.306
  8.0 0.1 fusion.36
  8.1 0.1 reduce_window_sum.11
  8.2 0.2 select_reduce_fusion.1
  8.4 0.1 sub.24
  8.5 0.7 multiply_add_fusion
  9.2 0.1 fusion.35
  9.3 2.5 convolution_convert_fusion.1
  11.8 2.6 reshape.273
  14.5 56.6 %all_to_all.15 = bf16[32,3,7168]{2,1,0:T(4,128)(2,1)} all-to-all(bf16[32,3,7168]{2,1,0:T(4,128)(2,1)S(1)} %reshape.273), channel_id=1, replica_groups=mesh['req'=8,'ep'=32] {'ep'}, dimensions={0} | all-to-all | bytes 2752512 | tf_op jit(solution)/shard_map/all_to_all | solution.py:118
  71.1 3.0 stack_reshape.2
  74.1 5.5 %stack.3 = bf16[8,96,7168]{2,1,0:T(8,128)(2,1)} broadcast(bf16[96,7168]{1,0:T(8,128)(2,1)S(1)} %stack_reshape.2), dimensions={1,2} | broadcast | bytes 12386304 | tf_op jit(solution)/shard_map/stack | solution.py:122
  79.6 129.2 %all_to_all.16 = bf16[8,96,7168]{2,1,0:T(8,128)(2,1)S(1)} all-to-all(bf16[8,96,7168]{2,1,0:T(8,128)(2,1)} %stack.3), channel_id=1, replica_groups=mesh['req'=8,'ep'=32] {'req'}, dimensions={0} | all-to-all | bytes 22020096 | tf_op jit(solution)/shard_map/all_to_all | solution.py:121
  208.8 4.0 %copy-done.1 = bf16[8,96,7168]{2,1,0:T(8,128)(2,1)} copy-done((bf16[8,96,7168]{2,1,0:T(8,128)(2,1)}, bf16[8,96,7168]{2,1,0:T(8,128)(2,1)S(1)}, u32[]{:S(2)}) %copy-start.1) | copy-done | bytes 11010072
  212.8 3.0 fusion.3
  215.8 18.9 %convolution_convert_fusion = bf16[768,7168]{1,0:T(8,128)(2,1)} fusion(bf16[1,256,7168]{2,1,0:T(8,128)(2,1)} %param.21, bf16[768,7168]{1,0:T(8,128)(2,1)} %bitcast.101, bf16[1,7168,256]{2,1,0:T(8,128)(2,1)} %param.20, f32[768,256]{1,0:T(8,128)S(1)} %fusion.3), kind=kOutput, calls=%fused_computation.16 | convolution fusion | flops 5643829248 | bytes 30146560 | tf_op jit(solution)/shard_map/dot_general | solution.py:36
  234.8 0.7 copy-done.7
  235.5 0.3 collective-permute-start.1
  235.8 1.7 collective-permute-start
  237.5 0.6 dynamic_slice.11
  238.1 0.2 dynamic-slice_reduce_fusion
  238.3 0.7 gather_fusion
  239.0 0.7 gather_fusion.1
  239.7 0.7 gather_fusion.2
  240.3 0.7 gather_fusion.3
  241.0 0.7 gather_fusion.4
  241.7 0.7 gather_fusion.5
  242.4 0.7 gather_fusion.6
  243.1 0.7 gather_fusion.7
  243.8 0.7 gather_fusion.8
  244.4 0.7 gather_fusion.9
  245.1 0.7 gather_fusion.10
  245.8 0.7 gather_fusion.11
  246.5 0.1 dynamic-slice
  246.6 0.7 gather_fusion.12
  247.2 0.1 dynamic-slice.1
  247.3 0.7 gather_fusion.13
  248.0 0.1 dynamic-slice.2
  248.1 0.7 gather_fusion.14
  248.7 0.1 dynamic-slice.3
  248.8 0.7 gather_fusion.15
  249.5 0.1 dynamic-slice.4
  249.6 0.7 iota_compare_fusion.19
  250.2 0.1 iota_compare_fusion.2
  250.3 0.1 fusion.51
  250.4 46.4 %reduce-scatter.2.cloned.1.call-done = bf16[96,7168]{1,0:T(8,128)(2,1)} async-done(((bf16[768,7168]{1,0:T(8,128)(2,1)}), bf16[96,7168]{1,0:T(8,128)(2,1)}) %reduce-scatter.2.cloned.1.call-update) | async-done | bytes 1376272 | tf_op jit(solution)/shard_map/reduce_scatter | solution.py:135
  296.8 4.0 %convert_element_type.37 = bf16[32,3,7168]{2,1,0:T(4,128)(2,1)} reshape(bf16[96,7168]{1,0:T(8,128)(2,1)} %reduce-scatter.2.cloned.1.call-done) | data formatting | bytes 2752512 | tf_op jit(solution)/shard_map/convert_element_type | solution.py:143
  300.8 10.2 %all-to-all-start.2 = ((bf16[32,3,7168]{2,1,0:T(4,128)(2,1)}), bf16[32,3,7168]{2,1,0:T(4,128)(2,1)S(1)}, u32[]{:S(2)}, u32[]{:S(2)}) async-start(bf16[32,3,7168]{2,1,0:T(4,128)(2,1)} %convert_element_type.37), calls=%async_computation.3 | async-start | bytes 3670016 | tf_op jit(solution)/shard_map/all_to_all | solution.py:142
  311.0 0.1 reduce_sum.38
  311.1 0.1 multiply_divide_fusion
  311.2 0.7 select_reduce_fusion
  311.9 1.4 copy.28
  313.2 1.0 broadcast_in_dim.21
  314.2 2.4 copy.32
  316.7 2.2 copy.29
  318.8 1.3 select_bitcast_fusion.1
  320.2 1.2 fusion.70
  321.4 0.4 fusion.7
  321.7 0.4 divide_convert_fusion
  322.1 1.4 copy.33
  323.5 3.2 convolution_convert_fusion.3
  326.7 28.4 %all-to-all-done.2 = bf16[32,3,7168]{2,1,0:T(4,128)(2,1)S(1)} async-done(((bf16[32,3,7168]{2,1,0:T(4,128)(2,1)}), bf16[32,3,7168]{2,1,0:T(4,128)(2,1)S(1)}, u32[]{:S(2)}, u32[]{:S(2)}) %all-to-all-start.2) | async-done | bytes 1376288 | tf_op jit(solution)/shard_map/all_to_all | solution.py:142
  355.1 2.4 reshape.275
  357.4 2.6 convolution_convert_fusion.2
  (64 shorter events, 0.4 us)
Async XLA Ops:
  7.2 313.0 %copy-start = (bf16[8,64,576]{2,1,0:T(8,128)(2,1)S(1)}, bf16[8,64,576]{2,1,0:T(8,128)(2,1)}, u32[]{:S(2)}) copy-start(bf16[8,64,576]{2,1,0:T(8,128)(2,1)} %param.11) | copy-start | bytes 1769476
  7.2 289.6 %reduce-scatter.2.cloned.1.call-start = ((), (), s32[]{:S(2)}) async-start(), calls=%async_computation.4 | async-start | bytes 12386304 | tf_op jit(solution)/shard_map/reduce_scatter | solution.py:135
  79.6 133.2 %copy-start.11 = (bf16[1,7168,256]{2,1,0:T(8,128)(2,1)S(1)}, bf16[1,7168,256]{2,1,0:T(8,128)(2,1)}, u32[]{:S(2)}) copy-start(bf16[1,7168,256]{2,1,0:T(8,128)(2,1)} %param.19) | copy-start | bytes 11010052
  208.8 4.0 %copy-start.1 = (bf16[8,96,7168]{2,1,0:T(8,128)(2,1)}, bf16[8,96,7168]{2,1,0:T(8,128)(2,1)S(1)}, u32[]{:S(2)}) copy-start(bf16[8,96,7168]{2,1,0:T(8,128)(2,1)S(1)} %all_to_all.16) | copy-start | bytes 33030148
  234.8 0.7 copy-start.7
  234.8 2.7 copy-start.12
  234.8 3.3 copy-start.10
  235.5 81.2 %collective-permute-start.1 = (bf16[8,576]{1,0:T(8,128)(2,1)S(1)}, bf16[8,576]{1,0:T(8,128)(2,1)S(1)}, u32[]{:S(2)}, u32[]{:S(2)}) collective-permute-start(bf16[8,576]{1,0:T(8,128)(2,1)S(1)} %copy-done.7), channel_id=1, source_target_pairs={{0,1},{1,0},{2,3},{3,2},{4,5},{5,4},{6,7},{7,6},{8,9},{9,8},{10,11... | collective-permute-start | bytes 27656 | tf_op jit(solution)/shard_map/ppermute | solution.py:18
  235.8 80.9 %collective-permute-start = (bf16[1,512,576]{1,2,0:T(8,128)(2,1)}, bf16[1,512,576]{1,2,0:T(8,128)(2,1)}, u32[]{:S(2)}, u32[]{:S(2)}) collective-permute-start(bf16[1,512,576]{1,2,0:T(8,128)(2,1)} %param.12), channel_id=1, source_target_pairs={{0,1},{1,0},{2,3},{3,2},{4,5},{5,4},{6,7},{7,6},{8,9},{9,8},{10,11... | collective-permute-start | bytes 1769480 | tf_op jit(solution)/shard_map/ppermute | solution.py:18
  300.8 10.2 %copy-start.6 = (f32[8,8]{1,0:T(8,128)S(1)}, f32[8,8]{1,0:T(8,128)}, u32[]{:S(2)}) copy-start(f32[8,8]{1,0:T(8,128)} %param.18) | copy-start | bytes 772
  300.8 54.3 %all-to-all-start.2 = ((bf16[32,3,7168]{2,1,0:T(4,128)(2,1)}), bf16[32,3,7168]{2,1,0:T(4,128)(2,1)S(1)}, u32[]{:S(2)}, u32[]{:S(2)}) async-start(bf16[32,3,7168]{2,1,0:T(4,128)(2,1)} %convert_element_type.37), calls=%async_computation.3 | async-start | bytes 3670016 | tf_op jit(solution)/shard_map/all_to_all | solution.py:142
  316.7 4.7 %copy-start.8 = (bf16[8,576]{1,0:T(8,128)(2,1)}, bf16[8,576]{1,0:T(8,128)(2,1)S(1)}, u32[]{:S(2)}) copy-start(bf16[8,576]{1,0:T(8,128)(2,1)S(1)} %get-tuple-element.4) | copy-start | bytes 27652
  316.7 4.7 %copy-start.9 = (bf16[8,576]{1,0:T(8,128)(2,1)}, bf16[8,576]{1,0:T(8,128)(2,1)S(1)}, u32[]{:S(2)}) copy-start(bf16[8,576]{1,0:T(8,128)(2,1)S(1)} %get-tuple-element.5) | copy-start | bytes 27652
  318.8 1.3 copy-start.4
  320.1 1.2 copy-start.2
  320.1 1.2 copy-start.3
  326.7 30.7 %copy-start.5 = (f32[96,8]{0,1:T(8,128)S(1)}, f32[96,8]{0,1:T(8,128)}, u32[]{:S(2)}) copy-start(f32[96,8]{0,1:T(8,128)} %select_reduce_fusion) | copy-start | bytes 9220
Sparse Core Ops, SparseCore 0:
  234.9 61.8 reduce-scatter.1
